TPU v7x, 256 devices: a whole 4x4x8 slice. The times are simulated.
256 devices in a mesh: dp: 8 (over y, core), lang: 32 (over x, z).
Axes of the slice: x: 4, y: 4, z: 8, core: 2. Of those that a mesh axis runs over, the one named last changes fastest.
Arguments:
- inputs: bfloat16 [32768, 2048], P(('dp', 'lang')), may hold values from -6 to 6
- grad_out: bfloat16 [32768, 2048], P(('dp', 'lang')), may hold values from -6 to 6
- lang_ids: int32 [32768], P(('dp', 'lang')), may hold values from 0 to 199, as said below
- lang_block: int32 [200], replicated, may hold values from 0 to 31, as said below
- block_owner: int32 [32], replicated, may hold values from 0 to 31, each once
- w_in: bfloat16 [32, 4096, 2048], P('lang', 'dp'), may hold values from -0.125 to 0.125
- w_out: bfloat16 [32, 4096, 2048], P('lang', 'dp'), may hold values from -0.09375 to 0.09375
Outputs:
- grad_in: bfloat16 [32768, 2048], P(('dp', 'lang'))
- grad_w_in: bfloat16 [32, 4096, 2048], P('lang', 'dp')
- grad_w_out: bfloat16 [32, 4096, 2048], P('lang', 'dp')
Inputs may be any that keep to these rules, and one draw needn't show every extreme that they name: `lang_ids`: through lang_block, the 128 rows of one device name any one block at most 5 times; in every draw one block is named exactly 5 times by the rows of every device. `lang_block`: every block has at least one language. A permutation: block b's weights and gradients sit at index block_owner[b] of the block dimension.
All inputs are finite; a program needn't handle non-finite values.
Results may differ from a plain program's by a relative error of at most 0.019.
Values may be sent and summed in bfloat16 or wider, within the bound.
A program may use at most 128 MiB of HBM per device.

v0:
```python
import math
import jax
import jax.numpy as jnp
from jax import lax
from jax.sharding import PartitionSpec as P

gelu_scale = math.sqrt(2.0 / math.pi)
CAP = 5


def gelu_parts(pre_act):
    tanh_arg = gelu_scale * (pre_act + 0.044715 * pre_act * pre_act * pre_act)
    tangent = jnp.tanh(tanh_arg)
    gelu_value = 0.5 * pre_act * (1.0 + tangent)
    gelu_slope = 0.5 * (1.0 + tangent) + 0.5 * pre_act * (1.0 - tangent * tangent) * gelu_scale * (
        1.0 + 3.0 * 0.044715 * pre_act * pre_act
    )
    return (gelu_value, gelu_slope)


def local_grads(rows_x, rows_g, w_first, w_second):
    pre_act = jnp.dot(rows_x, w_first.T, preferred_element_type=jnp.float32)
    gelu_value, gelu_slope = gelu_parts(pre_act)
    activated = gelu_value.astype(jnp.bfloat16)
    back_grad = jnp.dot(rows_g, w_second.T, preferred_element_type=jnp.float32)
    pre_grad = (back_grad * gelu_slope).astype(jnp.bfloat16)
    g_out = jnp.dot(activated.T, rows_g, preferred_element_type=jnp.float32).astype(jnp.bfloat16)
    g_in = jnp.dot(pre_grad.T, rows_x, preferred_element_type=jnp.float32).astype(jnp.bfloat16)
    return (pre_grad, g_in, g_out)


def slots_of(lang_ids, lang_block, block_owner):
    rows = lang_ids.shape[0]
    holder_of_lang = jnp.sum(
        jnp.where(
            lang_block[:, None] == jnp.arange(block_owner.shape[0])[None, :],
            block_owner[None, :],
            0,
        ),
        axis=1,
    )
    holder = jnp.sum(
        jnp.where(
            lang_ids[:, None] == jnp.arange(lang_block.shape[0])[None, :],
            holder_of_lang[None, :],
            0,
        ),
        axis=1,
    )
    row = jnp.arange(rows)
    earlier = jnp.sum(
        ((holder[:, None] == holder[None, :]) & (row[None, :] < row[:, None])).astype(jnp.int32),
        axis=1,
    )
    return holder * CAP + earlier


def body(inputs, grad_out, lang_ids, lang_block, block_owner, w_in, w_out):
    feat = inputs.shape[1]
    n_lang = lax.axis_size("lang")
    slots = n_lang * CAP
    position = slots_of(lang_ids, lang_block, block_owner)
    onehot = (position[None, :] == jnp.arange(slots)[:, None]).astype(jnp.bfloat16)
    packed = jnp.concatenate([inputs, grad_out], axis=1)
    outgoing = jnp.dot(onehot, packed, preferred_element_type=jnp.float32).astype(jnp.bfloat16)
    outgoing = outgoing.reshape(n_lang, CAP * 2 * feat // 128, 128)
    arrived = lax.all_to_all(outgoing, "lang", split_axis=0, concat_axis=0, tiled=True)
    arrived = arrived.reshape(slots, 2 * feat)
    gathered = lax.all_gather(arrived, "dp", axis=0, tiled=True)
    pre_grad, g_in, g_out = local_grads(gathered[:, :feat], gathered[:, feat:], w_in[0], w_out[0])
    partial_dx = jnp.dot(pre_grad, w_in[0], preferred_element_type=jnp.float32).astype(jnp.bfloat16)
    summed = lax.psum_scatter(partial_dx, "dp", scatter_dimension=0, tiled=True)
    back = summed.reshape(n_lang, CAP * feat // 128, 128)
    returned = lax.all_to_all(back, "lang", split_axis=0, concat_axis=0, tiled=True)
    returned = returned.reshape(slots, feat)
    grad_in = jnp.dot(onehot.T, returned, preferred_element_type=jnp.float32).astype(jnp.bfloat16)
    return (grad_in, g_in[None], g_out[None])


def solution(mesh):
    in_specs = (
        P(("dp", "lang"), None),
        P(("dp", "lang"), None),
        P(("dp", "lang")),
        P(),
        P(),
        P("lang", "dp", None),
        P("lang", "dp", None),
    )
    out_specs = (P(("dp", "lang"), None), P("lang", "dp", None), P("lang", "dp", None))
    return jax.shard_map(body, mesh=mesh, in_specs=in_specs, out_specs=out_specs, check_vma=False)
```

profile of v0, /device:TPU:32, one launch (start us, length us, event | category | flops | bytes accessed | tf_op | source)
XLA Modules:
  0.0 218.1 jit_solution(15846784867144905162)
XLA Ops:
  7.2 0.0 copy-start
  7.2 0.0 all-gather.2.cloned.1.call-start
  7.2 0.9 select_reduce_fusion.1
  8.2 0.8 select_reduce_fusion
  8.9 0.2 convert_reduce_fusion
  9.1 2.8 %convolution_convert_fusion.1 = bf16[160,4096]{1,0:T(8,128)(2,1)} fusion(bf16[128,2048]{1,0:T(8,128)(2,1)} %param.8, bf16[128,2048]{1,0:T(8,128)(2,1)} %param.7, s32[128]{0:T(128)S(1)} %multiply_add_fusion.1), kind=kOutput, calls=%fused_computation.1 | convolution fusion | flops 170545152 | bytes 2359808 | tf_op jit(solution)/shard_map/dot_general | solution.py:65
  11.9 2.4 %reshape.30 = bf16[32,160,128]{2,1,0:T(8,128)(2,1)S(1)} reshape(bf16[160,4096]{1,0:T(8,128)(2,1)} %convolution_convert_fusion.1) | data formatting | bytes 2621440 | tf_op jit(solution)/shard_map/reshape | solution.py:66
  14.3 45.8 %all_to_all.10 = bf16[32,160,128]{2,1,0:T(8,128)(2,1)} all-to-all(bf16[32,160,128]{2,1,0:T(8,128)(2,1)S(1)} %reshape.30), channel_id=1, replica_groups=mesh['dp'=8,'lang'=32] {'lang'}, dimensions={0} | all-to-all | bytes 2621440 | tf_op jit(solution)/shard_map/all_to_all | solution.py:67
  60.1 3.2 %reshape.31 = bf16[160,4096]{1,0:T(8,128)(2,1)} reshape(bf16[32,160,128]{2,1,0:T(8,128)(2,1)} %all_to_all.10) | data formatting | bytes 2621440 | tf_op jit(solution)/shard_map/reshape | solution.py:68
  63.3 0.0 all-gather.2.cloned.1.call-update
  63.3 0.0 reduce-scatter.2.cloned.1.call-start
  63.4 57.2 %all-gather.2.cloned.1.call-done = bf16[1280,4096]{1,0:T(8,128)(2,1)} async-done(((bf16[160,4096]{1,0:T(8,128)(2,1)}), bf16[1280,4096]{1,0:T(8,128)(2,1)}) %all-gather.2.cloned.1.call-update) | async-done | bytes 10485776 | tf_op jit(solution)/shard_map/all_gather | solution.py:69
  120.6 0.0 copy-done
  120.6 0.0 copy-start.1
  120.6 0.0 copy-start.2
  120.6 5.0 %fusion.2 = f32[1280,512]{1,0:T(8,128)S(1)} fusion(bf16[1280,4096]{1,0:T(8,128)(2,1)} %all-gather.2.cloned.1.call-done, bf16[1,512,2048]{2,1,0:T(8,128)(2,1)S(1)} %copy-done), kind=kOutput, calls=%fused_computation.4 | convolution fusion | flops 2684354560 | bytes 9961472 | tf_op jit(solution)/shard_map/dot_general | solution.py:22
  125.7 0.5 copy-done.1
  126.2 0.6 copy-done.2
  126.8 0.0 copy-start.3
  126.8 4.3 %fusion.11 = bf16[1280,512]{1,0:T(8,128)(2,1)S(1)} fusion(bf16[1280,4096]{1,0:T(8,128)(2,1)S(1)} %copy-done.1, f32[1280,512]{1,0:T(8,128)S(1)} %fusion.2, bf16[1,512,2048]{2,1,0:T(8,128)(2,1)S(1)} %copy-done.2), kind=kOutput, calls=%fused_computation.13 | convolution fusion | flops 2696806400 | bytes 11272192 | tf_op jit(solution)/shard_map/dot_general | solution.py:25
  131.1 0.0 copy-done.3
  131.1 0.0 copy-start.5
  131.1 1.0 copy-done.5
  132.1 4.7 %convolution_convert_fusion = bf16[1280,2048]{1,0:T(8,128)(2,1)} fusion(bf16[1280,512]{1,0:T(8,128)(2,1)S(1)} %fusion.11, bf16[1,512,2048]{2,1,0:T(8,128)(2,1)S(1)} %copy-done), kind=kOutput, calls=%fused_computation | convolution fusion | flops 2686976000 | bytes 8650752 | tf_op jit(solution)/shard_map/dot_general | solution.py:71
  136.8 0.0 reduce-scatter.2.cloned.1.call-update
  136.8 43.0 %reduce-scatter.2.cloned.1.call-done = bf16[160,2048]{1,0:T(8,128)(2,1)} async-done(((bf16[1280,2048]{1,0:T(8,128)(2,1)}), bf16[160,2048]{1,0:T(8,128)(2,1)}) %reduce-scatter.2.cloned.1.call-update) | async-done | bytes 655376 | tf_op jit(solution)/shard_map/reduce_scatter | solution.py:72
  179.8 2.1 reshape.32
  181.9 10.1 %all-to-all-start.1 = ((bf16[32,80,128]{2,1,0:T(8,128)(2,1)}), bf16[32,80,128]{2,1,0:T(8,128)(2,1)S(1)}, u32[]{:S(2)}, u32[]{:S(2)}) async-start(bf16[32,80,128]{2,1,0:T(8,128)(2,1)} %reshape.32), calls=%async_computation.2 | async-start | bytes 1310720 | tf_op jit(solution)/shard_map/all_to_all | solution.py:74
  192.0 0.0 copy-start.4
  192.0 7.3 %fusion.20 = bf16[1,512,2048]{2,1,0:T(8,128)(2,1)} fusion(bf16[1280,512]{1,0:T(8,128)(2,1)} %copy-done.5, bf16[1280,4096]{1,0:T(8,128)(2,1)} %all-gather.2.cloned.1.call-done), kind=kOutput, calls=%fused_computation.16 | convolution fusion | flops 2685403136 | bytes 8650752 | tf_op jit(solution)/shard_map/dot_general | solution.py:28
  199.3 0.0 copy-done.4
  199.3 6.7 %fusion.23 = bf16[1,512,2048]{2,1,0:T(8,128)(2,1)} fusion(bf16[1280,4096]{1,0:T(8,128)(2,1)} %all-gather.2.cloned.1.call-done, f32[1280,512]{1,0:T(8,128)S(1)} %copy-done.4), kind=kOutput, calls=%fused_computation.17 | convolution fusion | flops 2691301376 | bytes 9961472 | tf_op jit(solution)/shard_map/dot_general | solution.py:27
  206.0 3.8 %all-to-all-done.1 = bf16[32,80,128]{2,1,0:T(8,128)(2,1)S(1)} async-done(((bf16[32,80,128]{2,1,0:T(8,128)(2,1)}), bf16[32,80,128]{2,1,0:T(8,128)(2,1)S(1)}, u32[]{:S(2)}, u32[]{:S(2)}) %all-to-all-start.1) | async-done | bytes 655392 | tf_op jit(solution)/shard_map/all_to_all | solution.py:74
  209.8 0.3 reshape.33
  210.1 1.1 convolution_convert_fusion.2
  (1 shorter events, 0.0 us)
Async XLA Ops:
  7.2 113.5 %copy-start = (bf16[1,512,2048]{2,1,0:T(8,128)(2,1)S(1)}, bf16[1,512,2048]{2,1,0:T(8,128)(2,1)}, u32[]{:S(2)}) copy-start(bf16[1,512,2048]{2,1,0:T(8,128)(2,1)} %param.12) | copy-start | bytes 6291460
  7.2 113.4 %all-gather.2.cloned.1.call-start = ((), (), s32[]{:S(2)}) async-start(), calls=%async_computation.3 | async-start | bytes 11796480 | tf_op jit(solution)/shard_map/all_gather | solution.py:69
  63.3 116.5 %reduce-scatter.2.cloned.1.call-start = ((), (), s32[]{:S(2)}) async-start(), calls=%async_computation.4 | async-start | bytes 5898240 | tf_op jit(solution)/shard_map/reduce_scatter | solution.py:72
  120.6 5.5 %copy-start.1 = (bf16[1280,4096]{1,0:T(8,128)(2,1)S(1)}, bf16[1280,4096]{1,0:T(8,128)(2,1)}, u32[]{:S(2)}) copy-start(bf16[1280,4096]{1,0:T(8,128)(2,1)} %all-gather.2.cloned.1.call-done) | copy-start | bytes 31457284
  120.6 6.1 %copy-start.2 = (bf16[1,512,2048]{2,1,0:T(8,128)(2,1)S(1)}, bf16[1,512,2048]{2,1,0:T(8,128)(2,1)}, u32[]{:S(2)}) copy-start(bf16[1,512,2048]{2,1,0:T(8,128)(2,1)} %param.13) | copy-start | bytes 6291460
  126.8 4.3 %copy-start.3 = (f32[1280,512]{1,0:T(8,128)}, f32[1280,512]{1,0:T(8,128)S(1)}, u32[]{:S(2)}) copy-start(f32[1280,512]{1,0:T(8,128)S(1)} %fusion.2) | copy-start | bytes 7864324
  131.1 1.1 copy-start.5
  181.9 27.9 %all-to-all-start.1 = ((bf16[32,80,128]{2,1,0:T(8,128)(2,1)}), bf16[32,80,128]{2,1,0:T(8,128)(2,1)S(1)}, u32[]{:S(2)}, u32[]{:S(2)}) async-start(bf16[32,80,128]{2,1,0:T(8,128)(2,1)} %reshape.32), calls=%async_computation.2 | async-start | bytes 1310720 | tf_op jit(solution)/shard_map/all_to_all | solution.py:74
  192.0 7.3 %copy-start.4 = (f32[1280,512]{1,0:T(8,128)S(1)}, f32[1280,512]{1,0:T(8,128)}, u32[]{:S(2)}) copy-start(f32[1280,512]{1,0:T(8,128)} %copy-done.3) | copy-start | bytes 7864324
Sparse Core Ops, SparseCore 0:
  63.4 57.1 all-gather.1
  136.9 42.8 reduce-scatter.1
where the time goes:
time: 219 us; the launch traced here: 218 us
  waiting for transfers between devices  104 us (47%)
  blocking collectives  45.8 us (21%)
  matrix products  31.9 us (15%)
  between operations  14.1 us (6%)
  local copies, waits for them, and re-layouts  10.2 us (5%)
  starting transfers between devices  10.1 us (5%)
    all_gather x1, waiting for transfers between devices, body(): gathered = lax.all_gather(arrived, 'dp', axis=0, tiled=True)  57.2 us
    all_to_all x1, blocking collectives, body(): lax.all_to_all(outgoing, 'lang', split_axis=0, concat_axis=0, tiled=True)  45.8 us
    reduce_scatter x1, waiting for transfers between devices, body(): summed = lax.psum_scatter(partial_dx, 'dp', scatter_dimension=0, tiled=True)  43 us
    all_to_all x1, starting transfers between devices, body(): lax.all_to_all(back, 'lang', split_axis=0, concat_axis=0, tiled=True)  10.1 us
    dot_general x1, matrix products, local_grads(): jnp.dot(pre_grad.T, rows_x, preferred_element_type=jnp.float32)  7.27 us
    dot_general x1, matrix products, local_grads(): jnp.dot(activated.T, rows_g, preferred_element_type=jnp.float32)  6.74 us
    dot_general x1, matrix products, local_grads(): pre_act = jnp.dot(rows_x, w_first.T, preferred_element_type=jnp.float32)  5.03 us
    dot_general x1, matrix products, body(): jnp.dot(pre_grad, w_in[0], preferred_element_type=jnp.float32)  4.66 us
  transfers between devices with their start and end apart: 3, of which 3 were waited for; matrix products, arithmetic and copies ran while one was open for 6% of the time, Pallas kernels for 0%

commit v1 on v0

--- a/solution.py
+++ b/solution.py
@@ -3,6 +3,7 @@
 import jax.numpy as jnp
 from jax import lax
 from jax.sharding import PartitionSpec as P
+from jax.lax import all_to_all, psum
 
 gelu_scale = math.sqrt(2.0 / math.pi)
 CAP = 5
@@ -66,7 +67,9 @@
     outgoing = outgoing.reshape(n_lang, CAP * 2 * feat // 128, 128)
     arrived = lax.all_to_all(outgoing, "lang", split_axis=0, concat_axis=0, tiled=True)
     arrived = arrived.reshape(slots, 2 * feat)
-    gathered = lax.all_gather(arrived, "dp", axis=0, tiled=True)
+    gathered = jnp.concatenate(
+        all_to_all(jnp.stack([arrived for _ in range(psum(1, "dp"))]), "dp", 0, 0), axis=0
+    )
     pre_grad, g_in, g_out = local_grads(gathered[:, :feat], gathered[:, feat:], w_in[0], w_out[0])
     partial_dx = jnp.dot(pre_grad, w_in[0], preferred_element_type=jnp.float32).astype(jnp.bfloat16)
     summed = lax.psum_scatter(partial_dx, "dp", scatter_dimension=0, tiled=True)

time: 219 us -> 281 us (1.28)
  blocking collectives: 45.8 us -> 169 us
  waiting for transfers between devices: 104 us -> 40.4 us
  local copies, waits for them, and re-layouts: 10.2 us -> 14.8 us
    all_to_all x0 -> x1, blocking collectives: none -> 123 us  [body(): all_to_all(jnp.stack([arrived for _ in range(psum(1, 'dp'))]), 'dp', 0, 0)]
    all_gather x1 -> x0, waiting for transfers between devices: 57.2 us -> none  [body(): gathered = lax.all_gather(arrived, 'dp', axis=0, tiled=True)]
    another operation x0 -> x2, local copies, waits for them, and re-layouts: none -> 7.68 us  [body(): jnp.stack([arrived for _ in range(psum(1, 'dp'))])]
    reduce_scatter x1, waiting for transfers between devices: 43 us -> 36.6 us  [body(): summed = lax.psum_scatter(partial_dx, 'dp', scatter_dimension=0, tiled=True)]
    reshape x1 -> x0, local copies, waits for them, and re-layouts: 3.24 us -> none  [body(): arrived = arrived.reshape(slots, 2 * feat)]
  transfers between devices with their start and end apart: 3 -> 2, of which waited for: 3 -> 2; matrix products, arithmetic and copies ran while one was open for 6% -> 5% of each run, Pallas kernels for 0% -> 0%
where the time goes in v1:
time: 281 us; the launch traced here: 280 us
  blocking collectives  169 us (60%)
  waiting for transfers between devices  40.4 us (14%)
  matrix products  29.8 us (11%)
  local copies, waits for them, and re-layouts  14.8 us (5%)
  between operations  14.1 us (5%)
  starting transfers between devices  10.1 us (4%)
    all_to_all x1, blocking collectives, body(): all_to_all(jnp.stack([arrived for _ in range(psum(1, 'dp'))]), 'dp', 0, 0)  123 us
    all_to_all x1, blocking collectives, body(): lax.all_to_all(outgoing, 'lang', split_axis=0, concat_axis=0, tiled=True)  45.8 us
    reduce_scatter x1, waiting for transfers between devices, body(): summed = lax.psum_scatter(partial_dx, 'dp', scatter_dimension=0, tiled=True)  36.6 us
    all_to_all x1, starting transfers between devices, body(): lax.all_to_all(back, 'lang', split_axis=0, concat_axis=0, tiled=True)  10.1 us
    another operation x2, local copies, waits for them, and re-layouts, body(): jnp.stack([arrived for _ in range(psum(1, 'dp'))])  7.68 us
    dot_general x1, matrix products, local_grads(): jnp.dot(pre_grad.T, rows_x, preferred_element_type=jnp.float32)  7.27 us
    dot_general x1, matrix products, local_grads(): jnp.dot(activated.T, rows_g, preferred_element_type=jnp.float32)  6.81 us
  transfers between devices with their start and end apart: 2, of which 2 were waited for; matrix products, arithmetic and copies ran while one was open for 5% of the time, Pallas kernels for 0%

profile of v1, /device:TPU:32, one launch (start us, length us, event | category | flops | bytes accessed | tf_op | source)
XLA Modules:
  0.0 280.2 jit_solution(5785718043892843427)
XLA Ops:
  7.2 0.0 copy-start
  7.2 0.0 reduce-scatter.2.cloned.1.call-start
  7.2 0.9 select_reduce_fusion.1
  8.2 0.8 select_reduce_fusion
  8.9 0.2 convert_reduce_fusion
  9.1 2.8 convolution_convert_fusion.1
  11.9 2.4 reshape.32
  14.3 45.8 %all_to_all.15 = bf16[32,160,128]{2,1,0:T(8,128)(2,1)} all-to-all(bf16[32,160,128]{2,1,0:T(8,128)(2,1)S(1)} %reshape.32), channel_id=1, replica_groups=mesh['dp'=8,'lang'=32] {'lang'}, dimensions={0} | all-to-all | bytes 2621440 | tf_op jit(solution)/shard_map/all_to_all | solution.py:68
  60.1 2.4 stack_reshape.2
  62.4 5.3 %stack.3 = bf16[8,160,4096]{2,1,0:T(8,128)(2,1)} broadcast(bf16[160,4096]{1,0:T(8,128)(2,1)S(1)} %stack_reshape.2), dimensions={1,2} | broadcast | bytes 11796480 | tf_op jit(solution)/shard_map/stack | solution.py:71
  67.7 123.2 %all_to_all.16 = bf16[8,160,4096]{2,1,0:T(8,128)(2,1)S(1)} all-to-all(bf16[8,160,4096]{2,1,0:T(8,128)(2,1)} %stack.3), channel_id=1, replica_groups=mesh['dp'=8,'lang'=32] {'dp'}, dimensions={0} | all-to-all | bytes 20971520 | tf_op jit(solution)/shard_map/all_to_all | solution.py:71
  191.0 0.0 copy-start.1
  191.0 0.0 copy-done
  191.0 0.0 copy-start.2
  191.0 2.9 %fusion.2 = f32[1280,512]{1,0:T(8,128)S(1)} fusion(bf16[1280,4096]{1,0:T(8,128)(2,1)S(1)} %bitcast.16, bf16[1,512,2048]{2,1,0:T(8,128)(2,1)S(1)} %copy-done), kind=kOutput, calls=%fused_computation.4 | convolution fusion | flops 2684354560 | bytes 9961472 | tf_op jit(solution)/shard_map/dot_general | solution.py:23
  193.9 1.3 copy-done.1
  195.2 0.0 copy-done.2
  195.2 0.0 copy-start.3
  195.2 4.3 %fusion.11 = bf16[1280,512]{1,0:T(8,128)(2,1)S(1)} fusion(bf16[1280,4096]{1,0:T(8,128)(2,1)S(1)} %bitcast.17, f32[1280,512]{1,0:T(8,128)S(1)} %fusion.2, bf16[1,512,2048]{2,1,0:T(8,128)(2,1)S(1)} %copy-done.2), kind=kOutput, calls=%fused_computation.13 | convolution fusion | flops 2696806400 | bytes 11272192 | tf_op jit(solution)/shard_map/dot_general | solution.py:26
  199.5 0.0 copy-done.3
  199.5 0.0 copy-start.5
  199.5 1.0 copy-done.5
  200.6 4.6 %convolution_convert_fusion = bf16[1280,2048]{1,0:T(8,128)(2,1)} fusion(bf16[1280,512]{1,0:T(8,128)(2,1)S(1)} %fusion.11, bf16[1,512,2048]{2,1,0:T(8,128)(2,1)S(1)} %copy-done), kind=kOutput, calls=%fused_computation | convolution fusion | flops 2686976000 | bytes 8650752 | tf_op jit(solution)/shard_map/dot_general | solution.py:74
  205.2 0.0 reduce-scatter.2.cloned.1.call-update
  205.2 36.6 %reduce-scatter.2.cloned.1.call-done = bf16[160,2048]{1,0:T(8,128)(2,1)} async-done(((bf16[1280,2048]{1,0:T(8,128)(2,1)}), bf16[160,2048]{1,0:T(8,128)(2,1)}) %reduce-scatter.2.cloned.1.call-update) | async-done | bytes 655376 | tf_op jit(solution)/shard_map/reduce_scatter | solution.py:75
  241.8 2.2 reshape.34
  243.9 10.1 %all-to-all-start.2 = ((bf16[32,80,128]{2,1,0:T(8,128)(2,1)}), bf16[32,80,128]{2,1,0:T(8,128)(2,1)S(1)}, u32[]{:S(2)}, u32[]{:S(2)}) async-start(bf16[32,80,128]{2,1,0:T(8,128)(2,1)} %reshape.34), calls=%async_computation.3 | async-start | bytes 1310720 | tf_op jit(solution)/shard_map/all_to_all | solution.py:77
  254.0 0.0 copy-start.4
  254.0 7.3 %fusion.20 = bf16[1,512,2048]{2,1,0:T(8,128)(2,1)} fusion(bf16[1280,512]{1,0:T(8,128)(2,1)} %copy-done.5, bf16[1280,4096]{1,0:T(8,128)(2,1)} %bitcast.18), kind=kOutput, calls=%fused_computation.16 | convolution fusion | flops 2685403136 | bytes 8650752 | tf_op jit(solution)/shard_map/dot_general | solution.py:29
  261.3 0.0 copy-done.4
  261.3 6.8 %fusion.23 = bf16[1,512,2048]{2,1,0:T(8,128)(2,1)} fusion(bf16[1280,4096]{1,0:T(8,128)(2,1)} %bitcast.19, f32[1280,512]{1,0:T(8,128)S(1)} %copy-done.4), kind=kOutput, calls=%fused_computation.17 | convolution fusion | flops 2691301376 | bytes 9961472 | tf_op jit(solution)/shard_map/dot_general | solution.py:28
  268.1 3.8 %all-to-all-done.2 = bf16[32,80,128]{2,1,0:T(8,128)(2,1)S(1)} async-done(((bf16[32,80,128]{2,1,0:T(8,128)(2,1)}), bf16[32,80,128]{2,1,0:T(8,128)(2,1)S(1)}, u32[]{:S(2)}, u32[]{:S(2)}) %all-to-all-start.2) | async-done | bytes 655392 | tf_op jit(solution)/shard_map/all_to_all | solution.py:77
  271.9 0.3 reshape.35
  272.2 1.1 convolution_convert_fusion.2
  (1 shorter events, 0.0 us)
Async XLA Ops:
  7.2 183.8 %copy-start = (bf16[1,512,2048]{2,1,0:T(8,128)(2,1)S(1)}, bf16[1,512,2048]{2,1,0:T(8,128)(2,1)}, u32[]{:S(2)}) copy-start(bf16[1,512,2048]{2,1,0:T(8,128)(2,1)} %param.12) | copy-start | bytes 6291460
  7.2 234.6 %reduce-scatter.2.cloned.1.call-start = ((), (), s32[]{:S(2)}) async-start(), calls=%async_computation.4 | async-start | bytes 5898240 | tf_op jit(solution)/shard_map/reduce_scatter | solution.py:75
  191.0 4.2 %copy-start.1 = (bf16[8,160,4096]{2,1,0:T(8,128)(2,1)}, bf16[8,160,4096]{2,1,0:T(8,128)(2,1)S(1)}, u32[]{:S(2)}) copy-start(bf16[8,160,4096]{2,1,0:T(8,128)(2,1)S(1)} %all_to_all.16) | copy-start | bytes 31457284
  191.0 4.2 %copy-start.2 = (bf16[1,512,2048]{2,1,0:T(8,128)(2,1)S(1)}, bf16[1,512,2048]{2,1,0:T(8,128)(2,1)}, u32[]{:S(2)}) copy-start(bf16[1,512,2048]{2,1,0:T(8,128)(2,1)} %param.13) | copy-start | bytes 6291460
  195.2 4.3 %copy-start.3 = (f32[1280,512]{1,0:T(8,128)}, f32[1280,512]{1,0:T(8,128)S(1)}, u32[]{:S(2)}) copy-start(f32[1280,512]{1,0:T(8,128)S(1)} %fusion.2) | copy-start | bytes 7864324
  199.5 1.1 copy-start.5
  243.9 27.9 %all-to-all-start.2 = ((bf16[32,80,128]{2,1,0:T(8,128)(2,1)}), bf16[32,80,128]{2,1,0:T(8,128)(2,1)S(1)}, u32[]{:S(2)}, u32[]{:S(2)}) async-start(bf16[32,80,128]{2,1,0:T(8,128)(2,1)} %reshape.34), calls=%async_computation.3 | async-start | bytes 1310720 | tf_op jit(solution)/shard_map/all_to_all | solution.py:77
  254.0 7.3 %copy-start.4 = (f32[1280,512]{1,0:T(8,128)S(1)}, f32[1280,512]{1,0:T(8,128)}, u32[]{:S(2)}) copy-start(f32[1280,512]{1,0:T(8,128)} %copy-done.3) | copy-start | bytes 7864324
Sparse Core Ops, SparseCore 0:
  205.3 36.4 reduce-scatter.1
